TPU v7x, 128 devices: a whole 4x4x4 slice. The times are simulated.
128 devices in a mesh: row: 16 (over y, x), col: 8 (over z, core).
Axes of the slice: x: 4, y: 4, z: 4, core: 2. Of those that a mesh axis runs over, the one named last changes fastest.
Arguments:
- amplitudes: bfloat16 [192, 128, 1024], P('row', 'col'), may hold values from -6 to 6
- hole_int: bfloat16 [192, 192, 128, 128], P('row', None, 'col'), may hold values from -0.109375 to 0.109375
- ladder_int: bfloat16 [1024, 1024], replicated, may hold values from -0.5 to 0.5
- cycle_virt: bfloat16 [1024, 1024], replicated, may hold values from -0.5 to 0.5
- cycle_occ: bfloat16 [128, 128], replicated, may hold values from -0.5 to 0.5
- irrep_rows: int32 [192], replicated, may hold values from 0 to 7
- irrep_cols: int32 [128], replicated, may hold values from 0 to 7
- irrep_virt: int32 [1024], replicated, may hold values from 0 to 7
Outputs:
- residual: bfloat16 [192, 128, 1024], P('row', 'col')
All inputs are finite; a program needn't handle non-finite values.
Results may differ from a plain program's by a relative error of at most 0.014.
Values may be sent and summed in bfloat16 or wider, within the bound.
A program may use at most 128 MiB of HBM per device.

v0:
```python
import jax
import jax.numpy as jnp
from jax import lax
from jax.sharding import PartitionSpec as P


def local(
    amplitudes, hole_int, ladder_int, cycle_virt, cycle_occ, irrep_rows, irrep_cols, irrep_virt
):
    rows_own = amplitudes.shape[0]
    cols_own = amplitudes.shape[1]
    virt_width = amplitudes.shape[2]
    row_pos = lax.axis_index("row") * rows_own
    col_pos = lax.axis_index("col") * cols_own
    own_irrep = lax.dynamic_slice_in_dim(irrep_rows, row_pos, rows_own)
    own_cols = lax.dynamic_slice_in_dim(irrep_cols, col_pos, cols_own)
    sym_left = jnp.bitwise_xor(own_irrep[:, None], irrep_cols[None, :])
    sym_right = jnp.bitwise_xor(irrep_rows[:, None], own_cols[None, :])
    zero = jnp.zeros((), jnp.bfloat16)
    masked = jnp.where(sym_left[:, None, None, :] == sym_right[None, :, :, None], hole_int, zero)
    gathered = lax.all_gather(amplitudes, "row", axis=0, tiled=True)
    partial_value = jnp.einsum(
        "iklj,kla->ija", masked, gathered, preferred_element_type=jnp.float32
    )
    hole_own = lax.psum_scatter(
        partial_value.astype(jnp.bfloat16), "col", scatter_dimension=1, tiled=True
    ).astype(jnp.float32)
    same_irrep = irrep_virt[:, None] == irrep_virt[None, :]
    flat_amp = amplitudes.reshape(-1, virt_width)
    onebody = jnp.dot(
        flat_amp, jnp.where(same_irrep, ladder_int, zero), preferred_element_type=jnp.float32
    )
    middle = jnp.dot(
        flat_amp, jnp.where(same_irrep, cycle_virt, zero), preferred_element_type=jnp.float32
    )
    middle = middle.astype(jnp.bfloat16).reshape(amplitudes.shape)
    whole_mid = lax.all_gather(middle, "col", axis=1, tiled=True)
    occ_rows = lax.dynamic_slice_in_dim(cycle_occ, col_pos, cols_own, 0)
    cycle_term = jnp.einsum(
        "jl,ila->ija", occ_rows, whole_mid, preferred_element_type=jnp.float32
    ).astype(jnp.bfloat16)
    total = hole_own + onebody.reshape(hole_own.shape) + cycle_term.astype(jnp.float32)
    return total.astype(jnp.bfloat16)


def solution(mesh):
    placed = (P("row", "col", None), P("row", None, "col", None), P(), P(), P(), P(), P(), P())
    return jax.shard_map(
        local, mesh=mesh, in_specs=placed, out_specs=P("row", "col", None), check_vma=False
    )
```

profile of v0, /device:TPU:1, one launch (start us, length us, event | category | flops | bytes accessed | tf_op | source)
XLA Modules:
  0.0 148.1 jit_solution(6817195123913052483)
XLA Ops:
  6.5 0.0 copy-start
  6.5 0.0 copy-start.2
  6.5 0.0 copy-start.3
  6.5 0.0 all-gather.3.cloned.1.call-start
  6.5 0.7 all-gather.3.cloned.1.call-update
  7.3 0.0 all-gather.5.cloned.1.call-start
  7.3 3.3 %fusion.13 = bf16[1024,192]{0,1:T(8,128)(2,1)} fusion(bf16[192,1024]{1,0:T(8,128)(2,1)} %bitcast.28, bf16[1024,1024]{1,0:T(8,128)(2,1)} %param.11, s32[1024]{0:T(1024)} %param.15), kind=kOutput, calls=%fused_computation.15 | convolution fusion | flops 404946944 | bytes 2887680 | tf_op jit(solution)/shard_map/dot_general | solution.py:33
  10.6 0.0 all-gather.5.cloned.1.call-update
  10.6 0.0 reduce-scatter.2.cloned.1.call-start
  10.6 0.0 copy-done.2
  10.7 0.1 dynamic_slice.9
  10.7 0.0 copy-done.3
  10.7 0.1 dynamic_slice.10
  10.8 0.1 broadcast_xor_fusion.1
  10.9 0.1 broadcast_xor_fusion
  11.0 0.0 copy-start.1
  11.0 0.0 copy-start.4
  11.0 0.0 copy-start.5
  11.0 63.0 %all-gather.3.cloned.1.call-done = bf16[192,16,1024]{2,1,0:T(8,128)(2,1)} async-done(((bf16[12,16,1024]{2,1,0:T(8,128)(2,1)}), bf16[192,16,1024]{2,1,0:T(8,128)(2,1)}) %all-gather.3.cloned.1.call-update) | async-done | bytes 6291472 | tf_op jit(solution)/shard_map/all_gather | solution.py:21
  74.0 16.1 %bitcast_convert_fusion = bf16[12,128,1024]{2,1,0:T(8,128)(2,1)} fusion(bf16[192,16,1024]{2,1,0:T(8,128)(2,1)} %all-gather.3.cloned.1.call-done, bf16[12,192,16,128]{3,2,1,0:T(8,128)(2,1)} %param.9, s32[192,16]{1,0:T(8,128)S(1)} %broadcast_xor_fusion, s32[12,128]{1,0:T(8,128)S(1)} %broadcast_xor_fusion.1), kind=kOutput, calls=%fused_computation.4 | convolution fusion | flops 9674686464 | bytes 18892800 | tf_op jit(solution)/shard_map/iklj,kla->ija/dot_general | solution.py:22
  90.0 0.0 reduce-scatter.2.cloned.1.call-update
  90.1 0.0 copy-done.1
  90.1 0.0 copy-done.4
  90.1 0.0 copy-done.5
  90.1 0.9 fusion.7
  91.0 12.8 %all-gather.5.cloned.1.call-done = bf16[12,128,1024]{2,1,0:T(8,128)(2,1)} async-done(((bf16[12,16,1024]{2,1,0:T(8,128)(2,1)}), bf16[12,128,1024]{2,1,0:T(8,128)(2,1)}) %all-gather.5.cloned.1.call-update) | async-done | bytes 3145744 | tf_op jit(solution)/shard_map/all_gather | solution.py:37
  103.8 34.6 %reduce-scatter.2.cloned.1.call-done = bf16[12,16,1024]{2,1,0:T(8,128)(2,1)} async-done(((bf16[12,128,1024]{2,1,0:T(8,128)(2,1)}), bf16[12,16,1024]{2,1,0:T(8,128)(2,1)}) %reduce-scatter.2.cloned.1.call-update) | async-done | bytes 393232 | tf_op jit(solution)/shard_map/reduce_scatter | solution.py:25
  138.4 0.0 copy-done
  138.4 3.2 %fusion.17 = bf16[12,16,1024]{2,1,0:T(8,128)(2,1)} fusion(bf16[12,128,1024]{2,1,0:T(8,128)(2,1)} %all-gather.5.cloned.1.call-done, f32[12,16,1024]{2,1,0:T(8,128)S(1)} %bitcast.27, bf16[12,16,1024]{2,1,0:T(8,128)(2,1)} %reduce-scatter.2.cloned.1.call-done, bf16[128,128]{1,0:T(8,128)(2,1)S(1)} %copy-done, s32[]{:T(128)S(6)} %select_n.19), kind=kOutput, calls=%fused_computation.20 | convolution fusion | flops 51511296 | bytes 4722692 | tf_op jit(solution)/shard_map/jl,ila->ija/dot_general | solution.py:39
Async XLA Ops:
  6.5 131.8 %copy-start = (bf16[128,128]{1,0:T(8,128)(2,1)S(1)}, bf16[128,128]{1,0:T(8,128)(2,1)}, u32[]{:S(2)}) copy-start(bf16[128,128]{1,0:T(8,128)(2,1)} %param.12) | copy-start | bytes 98308
  6.5 4.1 %copy-start.2 = (s32[192]{0:T(256)S(1)}, s32[192]{0:T(256)}, u32[]{:S(2)}) copy-start(s32[192]{0:T(256)} %param.13) | copy-start | bytes 2308
  6.5 4.2 %copy-start.3 = (s32[128]{0:T(128)S(1)}, s32[128]{0:T(128)}, u32[]{:S(2)}) copy-start(s32[128]{0:T(128)} %param.14) | copy-start | bytes 1540
  6.5 67.4 %all-gather.3.cloned.1.call-start = ((), (), s32[]{:S(2)}) async-start(), calls=%async_computation.1 | async-start | bytes 6684672 | tf_op jit(solution)/shard_map/all_gather | solution.py:21
  7.3 96.5 %all-gather.5.cloned.1.call-start = ((), (), s32[]{:S(2)}) async-start(), calls=%async_computation.3 | async-start | bytes 3538944 | tf_op jit(solution)/shard_map/all_gather | solution.py:37
  10.6 127.8 %reduce-scatter.2.cloned.1.call-start = ((), (), s32[]{:S(2)}) async-start(), calls=%async_computation.2 | async-start | bytes 3538944 | tf_op jit(solution)/shard_map/reduce_scatter | solution.py:25
  11.0 79.1 %copy-start.1 = (bf16[12,16,1024]{2,1,0:T(8,128)(2,1)S(1)}, bf16[12,16,1024]{2,1,0:T(8,128)(2,1)}, u32[]{:S(2)}) copy-start(bf16[12,16,1024]{2,1,0:T(8,128)(2,1)} %param.8) | copy-start | bytes 1179652
  11.0 79.1 %copy-start.4 = (bf16[1024,1024]{1,0:T(8,128)(2,1)S(1)}, bf16[1024,1024]{1,0:T(8,128)(2,1)}, u32[]{:S(2)}) copy-start(bf16[1024,1024]{1,0:T(8,128)(2,1)} %param.10) | copy-start | bytes 6291460
  11.0 79.1 %copy-start.5 = (s32[1024]{0:T(1024)S(1)}, s32[1024]{0:T(1024)}, u32[]{:S(2)}) copy-start(s32[1024]{0:T(1024)} %param.15) | copy-start | bytes 12292
Sparse Core Ops, SparseCore 0:
  9.5 64.4 all-gather.2
  75.7 28.0 all-gather.4
  106.2 32.0 reduce-scatter.1
where the time goes:
time: 151 us; the launch traced here: 148 us
  waiting for transfers between devices  111 us (74%)
  matrix products  23.4 us (15%)
  between operations  13.2 us (9%)
    all_gather x1, waiting for transfers between devices, local(): gathered = lax.all_gather(amplitudes, 'row', axis=0, tiled=True)  63 us
    reduce_scatter x1, waiting for transfers between devices, local(): lax.psum_scatter(partial_value.astype(jnp.bfloat16), 'col', scatter_dimen...  34.6 us
    dot_general x1, matrix products, local(): jnp.einsum('iklj,kla->ija', masked, gathered, preferred_element_type=jnp....  16.1 us
    all_gather x1, waiting for transfers between devices, local(): whole_mid = lax.all_gather(middle, 'col', axis=1, tiled=True)  12.8 us
    dot_general x1, matrix products, local(): jnp.dot(flat_amp, jnp.where(same_irrep, cycle_virt, zero), preferred_elem...  3.26 us
    dot_general x1, matrix products, local(): jnp.einsum('jl,ila->ija', occ_rows, whole_mid, preferred_element_type=jnp...  3.24 us
  transfers between devices with their start and end apart: 3, of which 3 were waited for; matrix products, arithmetic and copies ran while one was open for 14% of the time, Pallas kernels for 0%

commit v1 on v0

v1 whole, which is shorter than its diff:
```python
import functools

import jax
import jax.numpy as jnp
from jax import lax
from jax.experimental import pallas as pl
from jax.experimental.pallas import tpu as pltpu
from jax.sharding import PartitionSpec as P

MESH = pl.DeviceIdType.MESH
BF, F32 = jnp.bfloat16, jnp.float32
SIDE = 4
ROWS, COLS, VIRT = 12, 16, 1024
OCC_I, OCC_J = 192, 128
HALF = ROWS * COLS // 2
PAIR = 2 * SIDE * HALF
WIDTHS = (256, 256, 256, 256)
STARTS = tuple(sum(WIDTHS[:c]) for c in range(len(WIDTHS)))
NCH = len(WIDTHS)
MT = 512
KINDS = 8


def kernel(t_hbm, x_hbm, f_hbm, u_hbm, z_ref, rows_s, cols_v, virt_v, out_hbm,
           tv, xraw, xt, fv, uv, dk, cs, vcol, bd, mid, ob, outv, *rest):
    n = NCH
    ts, accs, s1s, r1s, s2s, r2s, fins = (rest[i * n:(i + 1) * n] for i in range(7))
    (tsem, tvsem, xsem, fusem, osem, gs, gr, as_, ar, bs, br) = rest[7 * n:]
    row, col = lax.axis_index("row"), lax.axis_index("col")
    y, x = row // SIDE, row % SIDE
    z, core = col // 2, col % 2

    def axes(h):
        return (y, x) if h == 0 else (x, y)

    def dev(h, p, q):
        p, q = p % SIDE, q % SIDE
        return {"row": q * SIDE + p if h == 0 else p * SIDE + q, "col": col}

    def owner(h, g, m):
        return g * SIDE + m if h == 0 else m * SIDE + g

    zdev = lambda d: {"row": row, "col": (z + d) % SIDE * 2 + core}
    sibling = {"row": row, "col": col + 1 - 2 * core}

    tcopies = []
    for c in range(n):
        for h in range(2):
            q, p = axes(h)
            cp = pltpu.make_async_copy(
                t_hbm.at[pl.ds(h * HALF, HALF), pl.ds(STARTS[c], WIDTHS[c])], ts[c].at[h, q, p], tsem.at[c * 2 + h])
            cp.start()
            tcopies.append(cp)

    bar = pltpu.get_barrier_semaphore()
    for h in range(2):
        q, p = axes(h)
        for d in (1, 3):
            pl.semaphore_signal(bar, inc=1, device_id=dev(h, p + d, q), device_id_type=MESH)
    pl.semaphore_signal(bar, inc=1, device_id=sibling, device_id_type=MESH)
    for d in (1, 2, 3):
        pl.semaphore_signal(bar, inc=1, device_id=zdev(d), device_id_type=MESH)

    tvcopy = pltpu.make_async_copy(t_hbm, tv, tvsem.at[0])
    tvcopy.start()
    xcopies = {}
    for first in (True, False):
        for h in range(2):
            for o in range(2):
                q, _ = axes(h)
                pr = q // 2 if first else 1 - q // 2
                g = pr * 2 + o
                for m in range(SIDE):
                    r = owner(h, g, m)
                    cp = pltpu.make_async_copy(
                        x_hbm.at[:, pl.ds(r * 2 * HALF + h * HALF, HALF), :], xraw.at[h, g, :, m],
                        xsem.at[((first * 2 + h) * 2 + o) * SIDE + m])
                    cp.start()
                    xcopies[first, h, o, m] = cp
        if first:
            ucopy = pltpu.make_async_copy(u_hbm, uv, fusem.at[1])
            ucopy.start()
    fcopy = pltpu.make_async_copy(f_hbm, fv, fusem.at[0])
    fcopy.start()
    for cp in tcopies:
        cp.wait()
    pl.semaphore_wait(bar, 8)

    sends = []

    def rc(c, h, kind, d, ref):
        q, p = axes(h)
        s = 1 if d == 0 else 3
        to = dev(h, p + s, q) if kind < 2 else dev(h, p, q + s)
        i = ((c * 2 + h) * KINDS + kind) * 2 + d
        return pltpu.make_async_remote_copy(
            src_ref=ref, dst_ref=ref, send_sem=gs.at[i], recv_sem=gr.at[i], device_id=to, device_id_type=MESH)

    def send(*a):
        cp = rc(*a)
        cp.start()
        sends.append(cp)

    def wait(*a):
        rc(*a).wait_recv()

    OFF = {2: 0, 3: 3, 4: 1, 5: 2}
    FW = {0: (2, 4), 1: (3, 5)}

    def src(v, d):
        return (v + (3 if d == 0 else 1)) % SIDE

    def S(c):
        for kind in (0, 2):
            for h in range(2):
                q, p = axes(h)
                for d in range(2):
                    send(c, h, kind, d, ts[c].at[h, q, p])

    def E1(c):
        for h in range(2):
            q, p = axes(h)
            for d in range(2):
                r = src(p, d)
                wait(c, h, 0, d, ts[c].at[h, q, r])
                send(c, h, 1, d, ts[c].at[h, q, r, pl.ds(HALF // 2 * d, HALF // 2)])
        for h in range(2):
            q, p = axes(h)
            for k in (4, 3):
                for d in range(2):
                    send(c, h, k, d, ts[c].at[h, q, (p + OFF[k]) % SIDE])

    def E2(c):
        for h in range(2):
            q, p = axes(h)
            for d in range(2):
                wait(c, h, 1, d, ts[c].at[h, q, (p + 2) % SIDE, pl.ds(HALF // 2 * d, HALF // 2)])
            for d in range(2):
                send(c, h, 5, d, ts[c].at[h, q, (p + 2) % SIDE])

    def G(c, ks):
        for k in ks:
            for h in range(2):
                q, p = axes(h)
                for d in range(2):
                    r, m = src(q, d), (p + OFF[k]) % SIDE
                    wait(c, h, k, d, ts[c].at[h, r, m])
                    if k in FW[d]:
                        send(c, h, 6 + FW[d].index(k), d, ts[c].at[h, r, m])

    def H(c):
        for f in range(2):
            for h in range(2):
                q, p = axes(h)
                for d in range(2):
                    wait(c, h, 6 + f, d, ts[c].at[h, (q + 2) % SIDE, (p + OFF[FW[d][f]]) % SIDE])

    def prep():
        row_c = cols_v[...]
        cs[...] = jnp.broadcast_to(row_c, (OCC_J, OCC_J)).T
        base = cs[pl.ds(pl.multiple_of(col * COLS, COLS), COLS), :] ^ jnp.broadcast_to(row_c, (COLS, OCC_J))
        for h in range(2):
            def body(b, _, h=h):
                r = owner(h, b // SIDE, b % SIDE)
                for kk in range(ROWS // 2):
                    v = base ^ rows_s[r * ROWS + h * (ROWS // 2) + kk]
                    dk[h, b // SIDE, b % SIDE, kk * COLS:(kk + 1) * COLS, :] = v.astype(F32).astype(BF)
                return 0
            lax.fori_loop(0, SIDE * SIDE, body, 0)
        lane = lax.broadcasted_iota(jnp.int32, (OCC_J, ROWS * COLS), 1)
        sub = lax.broadcasted_iota(jnp.int32, (OCC_J, ROWS * COLS), 0)
        pick = jnp.where(sub == col * COLS + (lane & (COLS - 1)), 1.0, 0.0).astype(BF)
        tiled = jnp.dot(z_ref[...], pick, preferred_element_type=F32)
        for i in range(ROWS):
            bd[i * OCC_J:(i + 1) * OCC_J, :] = jnp.where((lane >> 4) == i, tiled, 0.0).astype(BF)
        for b in range(VIRT // 128):
            piece = virt_v[:, b * 128:(b + 1) * 128].astype(F32)
            vcol[b * 128:(b + 1) * 128, :] = jnp.broadcast_to(piece, (128, 128)).T.astype(BF)

    def build(first):
        for h in range(2):
            q, _ = axes(h)
            pr = q // 2 if first else 1 - q // 2
            for o in range(2):
                for m in range(SIDE):
                    xcopies[first, h, o, m].wait()
        def body(b, _):
            h, o = b // 2, b % 2
            q = y + h * (x - y)
            pr = q // 2 if first else 1 - q // 2
            g = pr * 2 + o
            start = pl.multiple_of((h * SIDE + g) * SIDE * HALF, SIDE * HALF)
            for i in range(ROWS):
                xs = xraw[h, g, i].reshape(SIDE * HALF, OCC_J)
                keep = dk[h, g].reshape(SIDE * HALF, OCC_J) == rows_s[row * ROWS + i].astype(F32).astype(BF)
                xs = jnp.where(keep, xs, jnp.zeros((), BF))
                xt[i * OCC_J:(i + 1) * OCC_J, pl.ds(start, SIDE * HALF)] = xs.T
            return 0
        lax.fori_loop(0, 4, body, 0)

    def mask_virt(w):
        def body(b, _):
            rows = pl.ds(pl.multiple_of(b * 128, 128), 128)
            for j in range(VIRT // 128):
                lanes = slice(j * 128, (j + 1) * 128)
                keep = vcol[rows, :] == virt_v[:, lanes].astype(F32).astype(BF)
                w[rows, lanes] = jnp.where(keep, w[rows, lanes], jnp.zeros((), BF))
            return 0
        lax.fori_loop(0, VIRT // 128, body, 0)

    def middle():
        ucopy.wait()
        tvcopy.wait()
        mask_virt(uv)
        def body(b, _):
            lanes = pl.ds(pl.multiple_of(b * 256, 256), 256)
            mid[:, lanes] = jnp.dot(tv[...], uv[:, lanes], preferred_element_type=F32).astype(BF)
            return 0
        lax.fori_loop(0, VIRT // 256, body, 0)

    def onebody():
        fcopy.wait()
        mask_virt(fv)
        def body(b, _):
            lanes = pl.ds(pl.multiple_of(b * 256, 256), 256)
            ob[:, lanes] = jnp.dot(tv[...], fv[:, lanes], preferred_element_type=F32)
            return 0
        lax.fori_loop(0, VIRT // 256, body, 0)

    def dots(c, first):
        w = WIDTHS[c]
        per = MT // OCC_J
        def body(mt, _):
            rows = pl.ds(pl.multiple_of(mt * MT, MT), MT)
            if first:
                total = jnp.dot(bd[rows, :], mid[:, STARTS[c]:STARTS[c] + w], preferred_element_type=F32)
            else:
                total = accs[c][pl.ds(mt * per, per)].reshape(MT, w)
            for h in range(2):
                q, _ = axes(h)
                pr = q // 2 if first else 1 - q // 2
                start = pl.multiple_of(h * 2 * PAIR + pr * PAIR, PAIR)
                block = ts[c][h, pl.ds(pr * 2, 2)].reshape(PAIR, w)
                total = total + jnp.dot(xt[rows, pl.ds(start, PAIR)], block, preferred_element_type=F32)
            accs[c][pl.ds(mt * per, per)] = total.reshape(per, SIDE, 2, COLS, w)
            return 0
        lax.fori_loop(0, ROWS * OCC_J // MT, body, 0)

    def to_sibling(c):
        return pltpu.make_async_remote_copy(
            src_ref=s1s[c], dst_ref=r1s[c], send_sem=as_.at[c], recv_sem=ar.at[c], device_id=sibling, device_id_type=MESH)

    def to_z(c, d):
        return pltpu.make_async_remote_copy(
            src_ref=s2s[c].at[d - 1], dst_ref=r2s[c].at[d - 1], send_sem=bs.at[c * 3 + d - 1], recv_sem=br.at[c * 3 + d - 1],
            device_id=zdev(d), device_id_type=MESH)

    def SA(c):
        s1s[c][...] = accs[c][:, :, 1 - core].astype(BF)
        to_sibling(c).start()

    def SB(c):
        w = WIDTHS[c]
        to_sibling(c).wait_recv()
        for d in (2, 1, 3):
            to = (z + d) % SIDE
            s2s[c][d - 1] = (accs[c][:, to, core] + r1s[c][:, to].astype(F32)).astype(BF)
            to_z(c, d).start()
        one = ob[:, STARTS[c]:STARTS[c] + w].reshape(ROWS, COLS, w)
        fins[c][...] = accs[c][:, z, core] + r1s[c][:, z].astype(F32) + one

    def out_copy(c):
        cols = pl.ds(STARTS[c], WIDTHS[c])
        return pltpu.make_async_copy(outv.at[:, :, cols], out_hbm.at[:, :, cols], osem.at[c])

    def SC(c):
        w = WIDTHS[c]
        for d in (1, 3, 2):
            to_z(c, d).wait_recv()
        total = fins[c][...]
        for d in (1, 2, 3):
            total = total + r2s[c][d - 1].astype(F32)
        outv[:, :, STARTS[c]:STARTS[c] + w] = total.astype(BF)
        out_copy(c).start()

    S(0); S(1)
    prep()
    build(True)
    E1(0); G(0, (2,))
    middle()
    E2(0); S(2); E1(1)
    build(False)
    G(0, (3, 4, 5)); E2(1); G(1, (2,))
    onebody()
    S(3); E1(2)
    dots(0, True)
    H(0); G(1, (3, 4, 5)); E2(2); G(2, (2,))
    dots(0, False); SA(0)
    E1(3)
    dots(1, True)
    H(1); G(2, (3, 4, 5)); E2(3); G(3, (2,))
    SB(0)
    dots(1, False); SA(1)
    dots(2, True)
    H(2); G(3, (3, 4, 5))
    SB(1)
    dots(2, False); SA(2)
    dots(3, True)
    SC(0); SB(2)
    H(3)
    dots(3, False); SA(3)
    SC(1); SB(3); SC(2); SC(3)
    for cp in sends:
        cp.wait_send()
    for c in range(n):
        to_sibling(c).wait_send()
        for d in (1, 2, 3):
            to_z(c, d).wait_send()
        out_copy(c).wait()


def local(amplitudes, hole_int, ladder_int, cycle_virt, cycle_occ, irrep_rows, irrep_cols, irrep_virt):
    vm, dma = pltpu.VMEM, pltpu.SemaphoreType.DMA
    any_, vspec = pl.BlockSpec(memory_space=pl.ANY), pl.BlockSpec(memory_space=pltpu.VMEM)
    scratch = [
        vm((ROWS * COLS, VIRT), BF), vm((2, SIDE, ROWS, SIDE, HALF, OCC_J), BF), vm((ROWS * OCC_J, OCC_I * COLS), BF),
        vm((VIRT, VIRT), BF), vm((VIRT, VIRT), BF), vm((2, SIDE, SIDE, HALF, OCC_J), BF), vm((OCC_J, OCC_J), jnp.int32),
        vm((VIRT, 128), BF), vm((ROWS * OCC_J, ROWS * COLS), BF), vm((ROWS * COLS, VIRT), BF), vm((ROWS * COLS, VIRT), F32),
        vm((ROWS, COLS, VIRT), BF),
    ]
    scratch += [vm((2, SIDE, SIDE, HALF, w), BF) for w in WIDTHS]
    scratch += [vm((ROWS, SIDE, 2, COLS, w), F32) for w in WIDTHS]
    scratch += [vm((ROWS, SIDE, COLS, w), BF) for w in WIDTHS]
    scratch += [vm((ROWS, SIDE, COLS, w), BF) for w in WIDTHS]
    scratch += [vm((SIDE - 1, ROWS, COLS, w), BF) for w in WIDTHS]
    scratch += [vm((SIDE - 1, ROWS, COLS, w), BF) for w in WIDTHS]
    scratch += [vm((ROWS, COLS, w), F32) for w in WIDTHS]
    ng = NCH * 2 * KINDS * 2
    scratch += [dma((NCH * 2,)), dma((1,)), dma((32,)), dma((2,)), dma((NCH,)), dma((ng,)), dma((ng,)),
                dma((NCH,)), dma((NCH,)), dma((NCH * 3,)), dma((NCH * 3,))]
    return pl.pallas_call(
        kernel,
        out_shape=jax.ShapeDtypeStruct((ROWS, COLS, VIRT), BF),
        in_specs=[any_, any_, any_, any_, vspec, pl.BlockSpec(memory_space=pltpu.SMEM), vspec, vspec],
        out_specs=any_,
        scratch_shapes=scratch,
        compiler_params=pltpu.CompilerParams(collective_id=0, has_side_effects=True, vmem_limit_bytes=60 * 2**20),
        name="residual",
    )(amplitudes.reshape(ROWS * COLS, VIRT), hole_int.reshape(ROWS, OCC_I * COLS, OCC_J), ladder_int, cycle_virt,
      cycle_occ, irrep_rows, irrep_cols.reshape(1, OCC_J), irrep_virt.reshape(1, VIRT))


def solution(mesh):
    placed = (P("row", "col", None), P("row", None, "col", None), P(), P(), P(), P(), P(), P())
    return jax.shard_map(
        local, mesh=mesh, in_specs=placed, out_specs=P("row", "col", None), check_vma=False
    )
```

time: 151 us -> 61.3 us (0.41); the launches traced: 148 us -> 61.1 us
  waiting for transfers between devices: 111 us -> 0 us
  Pallas kernels: 0 us -> 59.3 us
  matrix products: 23.4 us -> 0 us
  between operations: 13.2 us -> 0.01 us
  local copies, waits for them, and re-layouts: 0.18 us -> 1.77 us
    all_gather x2 -> x0, waiting for transfers between devices: 75.8 us -> none  [the longest x1 63 us: local(): gathered = lax.all_gather(amplitudes, 'row', axis=0, tiled=True)]
    pallas_call x0 -> x1, Pallas kernels: none -> 59.3 us  [local(): pl.pallas_call(kernel, out_shape=jax.ShapeDtypeStruct((ROWS, COLS, VIRT),...]
    reduce_scatter x1 -> x0, waiting for transfers between devices: 34.6 us -> none  [local(): lax.psum_scatter(partial_value.astype(jnp.bfloat16), 'col', scatter_dimen...]
    dot_general x4 -> x0, matrix products: 23.4 us -> none  [the longest x1 16.1 us: local(): jnp.einsum('iklj,kla->ija', masked, gathered, preferred_element_type=jnp....]
    unnamed x12 -> x1, local copies, waits for them, and re-layouts: 0.03 us -> 1.77 us
  transfers between devices with their start and end apart: 3 -> 0, of which waited for: 3 -> 0; matrix products, arithmetic and copies ran while one was open for 14% -> 0% of each run, Pallas kernels for 0% -> 0%
where the time goes in v1:
time: 61.3 us; the launch traced here: 61.1 us
  Pallas kernels  59.3 us (97%)
  local copies, waits for them, and re-layouts  1.77 us (3%)
    pallas_call x1, Pallas kernels, local(): pl.pallas_call(kernel, out_shape=jax.ShapeDtypeStruct((ROWS, COLS, VIRT),...  59.3 us
    unnamed x1, local copies, waits for them, and re-layouts  1.77 us

profile of v1, /device:TPU:1, one launch (start us, length us, event | category | flops | bytes accessed | tf_op | source)
XLA Modules:
  0.0 61.1 jit_solution(11008624938140685210)
XLA Ops:
  0.0 59.3 %residual.1 = bf16[12,16,1024]{2,1,0:T(8,128)(2,1)} custom-call(bf16[192,1024]{1,0:T(8,128)(2,1)} %bitcast.5, bf16[12,3072,128]{2,1,0:T(8,128)(2,1)} %bitcast.4, bf16[1024,1024]{1,0:T(8,128)(2,1)} %f_hbm.1, bf16[1024,1024]{1,0:T(8,128)(2,1)} %u_hbm.1, bf16[128,128]{1,0:T(8,128)(2,1)} %z_ref.1, s32[192]{0:T(256)} %rows_s.1, s32[1,128]{1,0:T(1,128)} %bitcast.7, ...), custom_call_target="tpu_custom_call" | custom-call | tf_op jit(solution)/shard_map/residual/pallas_call | solution.py:341
  59.3 1.8 %copy.10 = bf16[12,16,1024]{2,1,0:T(8,128)(2,1)} copy(bf16[12,16,1024]{2,1,0:T(8,128)(2,1)} %residual.1) | data formatting | bytes 786432

commit v2 on v1

v2 whole, which is shorter than its diff:
```python
import functools

import jax
import jax.numpy as jnp
from jax import lax
from jax.experimental import pallas as pl
from jax.experimental.pallas import tpu as pltpu
from jax.sharding import PartitionSpec as P

MESH = pl.DeviceIdType.MESH
BF, F32 = jnp.bfloat16, jnp.float32
SIDE = 4
ROWS, COLS, VIRT = 12, 16, 1024
OCC_I, OCC_J = 192, 128
HALF = ROWS * COLS // 2
WIDTHS = (256, 256, 256, 256)
STARTS = tuple(sum(WIDTHS[:c]) for c in range(len(WIDTHS)))
NCH = len(WIDTHS)
PARTS = (1, 1, 1, 2)
MT = 768
EVENTS = 8


SCHEDULE = (
    ('S', 0), ('S', 1), ('S', 2), ('prep',), ('build', True), ('E1', 0), ('G', 0, 2), ('onebody',), ('E1', 2), ('E2', 0), ('middle',), ('E1', 1), ('build', False), ('E2', 2), ('G', 0, 3, 4, 5), ('E2', 1), ('S', 3), ('G', 2, 2), ('dots', 0, 0), ('G', 2, 3, 4, 5), ('G', 1, 2), ('dots', 2, 0), ('G', 1, 3, 4, 5), ('dots', 1, 0), ('H', 0), ('E1', 3), ('dots', 0, 1), ('SA', 0), ('H', 2), ('dots', 2, 1), ('SA', 2), ('E2', 3), ('SB', 0), ('H', 1), ('dots', 1, 1), ('SA', 1), ('G', 3, 2), ('G', 3, 3, 4, 5), ('SB', 2), ('dots', 3, 0), ('SB', 1), ('dots', 3, 2), ('H', 3), ('dots', 3, 3, 0), ('SA', 3, 0), ('dots', 3, 3, 1), ('SA', 3, 1), ('SB', 3, 0), ('SB', 3, 1),
)


def kernel(t_hbm, x_hbm, f_hbm, u_hbm, z_hbm, rows_hbm, cols_hbm, virt_hbm, fin_hbm, r2_hbm,
           tv, xraw, xt, fv, uv, dk, cs, vcol, bd, mid, ob, finv, z_ref, cols_v, virt_v, rows_s, *rest):
    n = NCH
    ts, accs, s1s, r1s, s2s = (rest[i * n:(i + 1) * n] for i in range(5))
    (tsem, tvsem, xsem, fusem, osem, smsem, gs, gr, as_, ar, bs, br) = rest[5 * n:]
    row, col = lax.axis_index("row"), lax.axis_index("col")
    y, x = row // SIDE, row % SIDE
    z, core = col // 2, col % 2

    def axes(h):
        return (y, x) if h == 0 else (x, y)

    def dev(h, p, q):
        p, q = p % SIDE, q % SIDE
        return {"row": q * SIDE + p if h == 0 else p * SIDE + q, "col": col}

    def owner(h, g, m):
        return g * SIDE + m if h == 0 else m * SIDE + g

    zdev = lambda d: {"row": row, "col": (z + d) % SIDE * 2 + core}
    sibling = {"row": row, "col": col + 1 - 2 * core}

    small = []
    for i, (a, b) in enumerate(((rows_hbm, rows_s), (cols_hbm, cols_v), (z_hbm, z_ref), (virt_hbm, virt_v))):
        cp = pltpu.make_async_copy(a, b, smsem.at[i])
        small.append(cp)

    def block(h, g, m):
        return (h * SIDE + g) * SIDE + m

    for c in range(n):
        for h in range(2):
            q, p = axes(h)
            pltpu.make_async_copy(
                t_hbm.at[pl.ds(h * HALF, HALF), pl.ds(STARTS[c], WIDTHS[c])], ts[c].at[block(h, q, p)], tsem.at[0]).start()

    bar = pltpu.get_barrier_semaphore()
    for h in range(2):
        q, p = axes(h)
        for d in (1, 3):
            pl.semaphore_signal(bar, inc=1, device_id=dev(h, p + d, q), device_id_type=MESH)
    pl.semaphore_signal(bar, inc=1, device_id=sibling, device_id_type=MESH)
    for d in (1, 2, 3):
        pl.semaphore_signal(bar, inc=1, device_id=zdev(d), device_id_type=MESH)

    for cp in small:
        cp.start()
    tvcopy = pltpu.make_async_copy(t_hbm, tv, tvsem.at[0])
    tvcopy.start()
    ucopy = pltpu.make_async_copy(u_hbm, uv, fusem.at[1])
    fcopy = pltpu.make_async_copy(f_hbm, fv, fusem.at[0])
    for first in (True, False):
        for h in range(2):
            for o in range(2):
                q, _ = axes(h)
                g = (q // 2 if first else 1 - q // 2) * 2 + o
                for m in range(SIDE):
                    r = owner(h, g, m)
                    pltpu.make_async_copy(
                        x_hbm.at[:, pl.ds(r * 2 * HALF + h * HALF, HALF), :], xraw.at[h, g, :, m], xsem.at[1 - first]).start()
        if first:
            ucopy.start()
    fcopy.start()
    pltpu.make_async_copy(t_hbm, tv, tsem.at[0]).wait()
    pl.semaphore_wait(bar, 8)

    def send(c, h, kind, d, ref):
        q, p = axes(h)
        s = 1 if d == 0 else 3
        to = dev(h, p + s, q) if kind < 2 else dev(h, p, q + s)
        pltpu.make_async_remote_copy(
            src_ref=ref, dst_ref=ref, send_sem=gs.at[c], recv_sem=gr.at[c * EVENTS + kind], device_id=to,
            device_id_type=MESH).start()

    def arrived(c, kind, blocks):
        ref = ts[c].at[pl.ds(0, blocks)]
        pltpu.make_async_remote_copy(
            src_ref=ref, dst_ref=ref, send_sem=gs.at[c], recv_sem=gr.at[c * EVENTS + kind], device_id=sibling,
            device_id_type=MESH).wait_recv()

    OFF = {2: 0, 3: 3, 4: 1, 5: 2}
    FW = {0: (2, 4), 1: (3, 5)}

    def src(v, d):
        return (v + (3 if d == 0 else 1)) % SIDE

    def S(c):
        for kind in (0, 2):
            for h in range(2):
                q, p = axes(h)
                for d in range(2):
                    send(c, h, kind, d, ts[c].at[block(h, q, p)])

    def E1(c):
        arrived(c, 0, 4)
        for h in range(2):
            q, p = axes(h)
            for d in range(2):
                send(c, h, 1, d, ts[c].at[block(h, q, src(p, d)), pl.ds(HALF // 2 * d, HALF // 2)])
        for k in range(2):
            for h in range(2):
                q, p = axes(h)
                for d in range(2):
                    kind = (4, 3)[k ^ d]
                    send(c, h, kind, d, ts[c].at[block(h, q, (p + OFF[kind]) % SIDE)])

    def E2(c):
        arrived(c, 1, 2)
        for h in range(2):
            q, p = axes(h)
            for d in range(2):
                send(c, h, 5, d, ts[c].at[block(h, q, (p + 2) % SIDE)])

    def G(c, *ks):
        for k in ks or (2, 3, 4, 5):
            arrived(c, k, 4)
            d = 0 if k in FW[0] else 1
            for h in range(2):
                q, p = axes(h)
                send(c, h, 6 + FW[d].index(k), d, ts[c].at[block(h, src(q, d), (p + OFF[k]) % SIDE)])

    def H(c):
        arrived(c, 6, 4)
        arrived(c, 7, 4)

    def prep():
        small[1].wait()
        small[0].wait()
        row_c = cols_v[...]
        cs[...] = jnp.broadcast_to(row_c, (OCC_J, OCC_J)).T
        base = cs[pl.ds(pl.multiple_of(col * COLS, COLS), COLS), :] ^ jnp.broadcast_to(row_c, (COLS, OCC_J))
        for h in range(2):
            def body(b, _, h=h):
                r = owner(h, b // SIDE, b % SIDE)
                for kk in range(ROWS // 2):
                    v = base ^ rows_s[r * ROWS + h * (ROWS // 2) + kk]
                    dk[h, b // SIDE, b % SIDE, kk * COLS:(kk + 1) * COLS, :] = v.astype(F32).astype(BF)
                return 0
            lax.fori_loop(0, SIDE * SIDE, body, 0)
        small[2].wait()
        lane = lax.broadcasted_iota(jnp.int32, (OCC_J, ROWS * COLS), 1)
        sub = lax.broadcasted_iota(jnp.int32, (OCC_J, ROWS * COLS), 0)
        pick = jnp.where(sub == col * COLS + (lane & (COLS - 1)), 1.0, 0.0).astype(BF)
        tiled = jnp.dot(z_ref[...], pick, preferred_element_type=F32)
        for i in range(ROWS):
            bd[i * OCC_J:(i + 1) * OCC_J, :] = jnp.where((lane >> 4) == i, tiled, 0.0).astype(BF)
        small[3].wait()
        tvcopy.wait()
        for b in range(VIRT // 128):
            piece = virt_v[:, b * 128:(b + 1) * 128].astype(F32)
            vcol[b * 128:(b + 1) * 128, :] = jnp.broadcast_to(piece, (128, 128)).T.astype(BF)

    def build(first):
        pltpu.make_async_copy(x_hbm.at[pl.ds(0, ROWS // 2)], x_hbm.at[pl.ds(0, ROWS // 2)], xsem.at[1 - first]).wait()
        def body(b, _):
            h, o = b // 2, b % 2
            q = y + h * (x - y)
            pr = q // 2 if first else 1 - q // 2
            g = pr * 2 + o
            start = pl.multiple_of((h * SIDE + g) * SIDE * HALF, SIDE * HALF)
            for i in range(ROWS):
                xs = xraw[h, g, i].reshape(SIDE * HALF, OCC_J)
                keep = dk[h, g].reshape(SIDE * HALF, OCC_J) == rows_s[row * ROWS + i].astype(F32).astype(BF)
                xs = jnp.where(keep, xs, jnp.zeros((), BF))
                xt[i * OCC_J:(i + 1) * OCC_J, pl.ds(start, SIDE * HALF)] = xs.T
            return 0
        lax.fori_loop(0, 4, body, 0)

    def mask_virt(w):
        def body(b, _):
            rows = pl.ds(pl.multiple_of(b * 128, 128), 128)
            for j in range(VIRT // 128):
                lanes = slice(j * 128, (j + 1) * 128)
                keep = vcol[rows, :] == virt_v[:, lanes].astype(F32).astype(BF)
                w[rows, lanes] = jnp.where(keep, w[rows, lanes], jnp.zeros((), BF))
            return 0
        lax.fori_loop(0, VIRT // 128, body, 0)

    def middle():
        ucopy.wait()
        mask_virt(uv)
        def body(b, _):
            lanes = pl.ds(pl.multiple_of(b * 256, 256), 256)
            mid[:, lanes] = jnp.dot(tv[...], uv[:, lanes], preferred_element_type=F32).astype(BF)
            return 0
        lax.fori_loop(0, VIRT // 256, body, 0)

    def onebody():
        fcopy.wait()
        mask_virt(fv)
        def body(b, _):
            lanes = pl.ds(pl.multiple_of(b * 256, 256), 256)
            ob[:, lanes] = jnp.dot(tv[...], fv[:, lanes], preferred_element_type=F32)
            return 0
        lax.fori_loop(0, VIRT // 256, body, 0)

    def dots(c, groups, part=None):
        w = WIDTHS[c]
        per = MT // OCC_J

        def product(rows, h, start, count):
            ks = pl.ds(pl.multiple_of((h * SIDE + start) * SIDE * HALF, SIDE * HALF), count * SIDE * HALF)
            blocks = ts[c][pl.ds((h * SIDE + start) * SIDE, count * SIDE)].reshape(count * SIDE * HALF, w)
            return jnp.dot(xt[rows, ks], blocks, preferred_element_type=F32)

        def body(mt, _):
            rows = pl.ds(pl.multiple_of(mt * MT, MT), MT)
            if groups == 0:
                total = jnp.dot(bd[rows, :], mid[:, STARTS[c]:STARTS[c] + w], preferred_element_type=F32)
            else:
                total = accs[c][pl.ds(mt * per, per)].reshape(MT, w)
            for h in range(2):
                q, _ = axes(h)
                if groups < 2:
                    total = total + product(rows, h, (q // 2 if groups == 0 else 1 - q // 2) * 2, 2)
                else:
                    total = total + product(rows, h, 3 - q if groups == 2 else (q + 2) % SIDE, 1)
            accs[c][pl.ds(mt * per, per)] = total.reshape(per, SIDE, 2, COLS, w)
            return 0
        if part is None:
            lax.fori_loop(0, ROWS * OCC_J // MT, body, 0)
        else:
            body(part, 0)

    def share(c, part):
        size = ROWS // PARTS[c]
        return pl.ds(part * size, size)

    def to_sibling(c, part):
        i = share(c, part)
        return pltpu.make_async_remote_copy(
            src_ref=s1s[c].at[i], dst_ref=r1s[c].at[i], send_sem=as_.at[2 * c + part], recv_sem=ar.at[2 * c + part],
            device_id=sibling, device_id_type=MESH)

    def SA(c, part=0):
        i = share(c, part)
        s1s[c][i] = accs[c][i, :, 1 - core].astype(BF)
        to_sibling(c, part).start()

    def SB(c, part=0):
        w, i = WIDTHS[c], share(c, part)
        cols = pl.ds(STARTS[c], w)
        to_sibling(c, part).wait_recv()
        for d in (2, 1, 3):
            to = (z + d) % SIDE
            s2s[c][d - 1, i] = (accs[c][i, to, core] + r1s[c][i, to].astype(F32)).astype(BF)
            pltpu.make_async_remote_copy(
                src_ref=s2s[c].at[d - 1, i], dst_ref=r2_hbm.at[d - 1, i, :, cols], send_sem=bs.at[0], recv_sem=br.at[0],
                device_id=zdev(d), device_id_type=MESH).start()
        size = ROWS // PARTS[c]
        one = ob[part * size * COLS:(part + 1) * size * COLS, STARTS[c]:STARTS[c] + w].reshape(size, COLS, w)
        finv[i, :, cols] = accs[c][i, z, core] + r1s[c][i, z].astype(F32) + one
        pltpu.make_async_copy(finv.at[i, :, cols], fin_hbm.at[i, :, cols], osem.at[0]).start()

    for name, *args in SCHEDULE:
        dict(S=S, E1=E1, E2=E2, G=G, H=H, prep=prep, build=build, middle=middle, onebody=onebody, dots=dots, SA=SA, SB=SB)[name](*args)

    for c in range(n):
        ref = ts[c].at[pl.ds(0, 30)]
        pltpu.make_async_remote_copy(
            src_ref=ref, dst_ref=ref, send_sem=gs.at[c], recv_sem=gr.at[c], device_id=sibling, device_id_type=MESH).wait_send()
        for part in range(PARTS[c]):
            to_sibling(c, part).wait_send()
    pltpu.make_async_copy(finv, fin_hbm, osem.at[0]).wait()
    last = pltpu.make_async_remote_copy(
        src_ref=r2_hbm, dst_ref=r2_hbm, send_sem=bs.at[0], recv_sem=br.at[0], device_id=sibling, device_id_type=MESH)
    last.wait_send()
    last.wait_recv()


def local(amplitudes, hole_int, ladder_int, cycle_virt, cycle_occ, irrep_rows, irrep_cols, irrep_virt):
    vm, dma = pltpu.VMEM, pltpu.SemaphoreType.DMA
    any_ = pl.BlockSpec(memory_space=pl.ANY)
    scratch = [
        vm((ROWS * COLS, VIRT), BF), vm((2, SIDE, ROWS, SIDE, HALF, OCC_J), BF), vm((ROWS * OCC_J, OCC_I * COLS), BF),
        vm((VIRT, VIRT), BF), vm((VIRT, VIRT), BF), vm((2, SIDE, SIDE, HALF, OCC_J), BF), vm((OCC_J, OCC_J), jnp.int32),
        vm((VIRT, 128), BF), vm((ROWS * OCC_J, ROWS * COLS), BF), vm((ROWS * COLS, VIRT), BF), vm((ROWS * COLS, VIRT), F32),
        vm((ROWS, COLS, VIRT), F32), vm((OCC_J, OCC_J), BF), vm((1, OCC_J), jnp.int32), vm((1, VIRT), jnp.int32),
        pltpu.SMEM((OCC_I,), jnp.int32),
    ]
    scratch += [vm((2 * SIDE * SIDE, HALF, w), BF) for w in WIDTHS]
    scratch += [vm((ROWS, SIDE, 2, COLS, w), F32) for w in WIDTHS]
    scratch += [vm((ROWS, SIDE, COLS, w), BF) for w in WIDTHS]
    scratch += [vm((ROWS, SIDE, COLS, w), BF) for w in WIDTHS]
    scratch += [vm((SIDE - 1, ROWS, COLS, w), BF) for w in WIDTHS]
    scratch += [dma((k,)) for k in (1, 1, 2, 2, 1, 4, NCH, NCH * EVENTS, 2 * NCH, 2 * NCH, 1, 1)]
    own, others = pl.pallas_call(
        kernel,
        out_shape=(jax.ShapeDtypeStruct((ROWS, COLS, VIRT), F32), jax.ShapeDtypeStruct((SIDE - 1, ROWS, COLS, VIRT), BF)),
        in_specs=[any_] * 8,
        out_specs=(any_, any_),
        scratch_shapes=scratch,
        compiler_params=pltpu.CompilerParams(collective_id=0, has_side_effects=True, vmem_limit_bytes=60 * 2**20),
        name="residual",
    )(amplitudes.reshape(ROWS * COLS, VIRT), hole_int.reshape(ROWS, OCC_I * COLS, OCC_J), ladder_int, cycle_virt,
      cycle_occ, irrep_rows, irrep_cols.reshape(1, OCC_J), irrep_virt.reshape(1, VIRT))
    return (own + others[0].astype(F32) + others[1].astype(F32) + others[2].astype(F32)).astype(BF)


def solution(mesh):
    placed = (P("row", "col", None), P("row", None, "col", None), P(), P(), P(), P(), P(), P())
    return jax.shard_map(
        local, mesh=mesh, in_specs=placed, out_specs=P("row", "col", None), check_vma=False
    )
```

time: 61.3 us -> 57.1 us (0.931)
  Pallas kernels: 59.3 us -> 54.2 us
  other arithmetic: 0 us -> 2.46 us
  local copies, waits for them, and re-layouts: 1.77 us -> 0 us
    pallas_call x1, Pallas kernels: 59.3 us -> 54.2 us  [local(): pl.pallas_call(kernel, out_shape=(jax.ShapeDtypeStruct((ROWS, COLS, VIRT)...]
    convert_element_type x0 -> x1, other arithmetic: none -> 2.46 us  [local(): (own + others[0].astype(F32) + others[1].astype(F32) + others[2].astype(F...]
    unnamed x1 -> x0, local copies, waits for them, and re-layouts: 1.77 us -> none
where the time goes in v2:
time: 57.1 us; the launch traced here: 56.6 us
  Pallas kernels  54.2 us (95%)
  other arithmetic  2.46 us (4%)
    pallas_call x1, Pallas kernels, local(): pl.pallas_call(kernel, out_shape=(jax.ShapeDtypeStruct((ROWS, COLS, VIRT)...  54.2 us
    convert_element_type x1, other arithmetic, local(): (own + others[0].astype(F32) + others[1].astype(F32) + others[2].astype(F...  2.46 us

profile of v2, /device:TPU:1, one launch (start us, length us, event | category | flops | bytes accessed | tf_op | source)
XLA Modules:
  0.0 56.6 jit_solution(11142978073138422464)
XLA Ops:
  0.0 54.2 %residual.1 = (f32[12,16,1024]{2,1,0:T(8,128)}, bf16[3,12,16,1024]{3,2,1,0:T(8,128)(2,1)}) custom-call(bf16[192,1024]{1,0:T(8,128)(2,1)} %bitcast.14, bf16[12,3072,128]{2,1,0:T(8,128)(2,1)} %bitcast.13, bf16[1024,1024]{1,0:T(8,128)(2,1)} %f_hbm.1, bf16[1024,1024]{1,0:T(8,128)(2,1)} %u_hbm.1, bf16[128,128]{1,0:T(8,128)(2,1)} %z_hbm.1, s32[192]{0:T(256)} %rows_hbm.1, ...), custom_call_target="tpu_custom_call" | custom-call | tf_op jit(solution)/shard_map/residual/pallas_call | solution.py:315
  54.2 2.5 %fusion = bf16[12,16,1024]{2,1,0:T(8,128)(2,1)} fusion(f32[12,16,1024]{2,1,0:T(8,128)} %get-tuple-element.7, bf16[3,12,16,1024]{3,2,1,0:T(8,128)(2,1)} %get-tuple-element.8), kind=kLoop, calls=%fused_computation.1 | loop fusion | flops 1376256 | bytes 2359296 | tf_op jit(solution)/shard_map/convert_element_type | solution.py:325

commit v3 on v2

--- a/solution.py
+++ b/solution.py
@@ -16,13 +16,12 @@
 WIDTHS = (256, 256, 256, 256)
 STARTS = tuple(sum(WIDTHS[:c]) for c in range(len(WIDTHS)))
 NCH = len(WIDTHS)
-PARTS = (1, 1, 1, 2)
-MT = 768
+PARTS = (1, 1, 1, 4)
 EVENTS = 8
 
 
 SCHEDULE = (
-    ('S', 0), ('S', 1), ('S', 2), ('prep',), ('build', True), ('E1', 0), ('G', 0, 2), ('onebody',), ('E1', 2), ('E2', 0), ('middle',), ('E1', 1), ('build', False), ('E2', 2), ('G', 0, 3, 4, 5), ('E2', 1), ('S', 3), ('G', 2, 2), ('dots', 0, 0), ('G', 2, 3, 4, 5), ('G', 1, 2), ('dots', 2, 0), ('G', 1, 3, 4, 5), ('dots', 1, 0), ('H', 0), ('E1', 3), ('dots', 0, 1), ('SA', 0), ('H', 2), ('dots', 2, 1), ('SA', 2), ('E2', 3), ('SB', 0), ('H', 1), ('dots', 1, 1), ('SA', 1), ('G', 3, 2), ('G', 3, 3, 4, 5), ('SB', 2), ('dots', 3, 0), ('SB', 1), ('dots', 3, 2), ('H', 3), ('dots', 3, 3, 0), ('SA', 3, 0), ('dots', 3, 3, 1), ('SA', 3, 1), ('SB', 3, 0), ('SB', 3, 1),
+    ('D1', 0), ('O', 0), ('D1', 1), ('D1', 2), ('prep',), ('build', True), ('E1', 0), ('D1', 3), ('N', 0), ('middle',), ('E1', 1), ('E2', 0), ('N', 1), ('build', False), ('O', 1), ('G', 0, 3), ('G', 0, 4), ('G', 0, 2), ('onebody',), ('G', 0, 5), ('E2', 1), ('E1', 2), ('dots', 0, 0), ('O', 2), ('G', 1, 2), ('N', 2), ('G', 1, 3), ('G', 1, 4), ('H', 0), ('dots', 0, 1), ('G', 1, 5), ('E2', 2), ('SA', 0), ('E1', 3), ('dots', 1, 0), ('N', 3), ('SB', 0), ('G', 2, 3), ('G', 2, 4), ('G', 2, 2), ('H', 1), ('dots', 1, 1), ('G', 2, 5), ('O', 3), ('SA', 1), ('E2', 3), ('dots', 2, 0), ('G', 3, 4), ('G', 3, 3), ('SB', 1), ('H', 2), ('dots', 2, 1), ('G', 3, 2), ('SA', 2), ('G', 3, 5), ('dots', 3, 0), ('SB', 2), ('dots', 3, 2), ('H', 3), ('dots', 3, 3, 0), ('SA', 3, 0), ('dots', 3, 3, 1), ('SA', 3, 1), ('dots', 3, 3, 2), ('SA', 3, 2), ('dots', 3, 3, 3), ('SA', 3, 3), ('SB', 3, 0), ('SB', 3, 1), ('SB', 3, 2), ('SB', 3, 3),
 )
 
 
@@ -56,12 +55,6 @@
     def block(h, g, m):
         return (h * SIDE + g) * SIDE + m
 
-    for c in range(n):
-        for h in range(2):
-            q, p = axes(h)
-            pltpu.make_async_copy(
-                t_hbm.at[pl.ds(h * HALF, HALF), pl.ds(STARTS[c], WIDTHS[c])], ts[c].at[block(h, q, p)], tsem.at[0]).start()
-
     bar = pltpu.get_barrier_semaphore()
     for h in range(2):
         q, p = axes(h)
@@ -71,33 +64,40 @@
     for d in (1, 2, 3):
         pl.semaphore_signal(bar, inc=1, device_id=zdev(d), device_id_type=MESH)
 
-    for cp in small:
-        cp.start()
     tvcopy = pltpu.make_async_copy(t_hbm, tv, tvsem.at[0])
-    tvcopy.start()
     ucopy = pltpu.make_async_copy(u_hbm, uv, fusem.at[1])
     fcopy = pltpu.make_async_copy(f_hbm, fv, fusem.at[0])
-    for first in (True, False):
-        for h in range(2):
-            for o in range(2):
-                q, _ = axes(h)
-                g = (q // 2 if first else 1 - q // 2) * 2 + o
-                for m in range(SIDE):
-                    r = owner(h, g, m)
-                    pltpu.make_async_copy(
-                        x_hbm.at[:, pl.ds(r * 2 * HALF + h * HALF, HALF), :], xraw.at[h, g, :, m], xsem.at[1 - first]).start()
-        if first:
-            ucopy.start()
-    fcopy.start()
-    pltpu.make_async_copy(t_hbm, tv, tsem.at[0]).wait()
+
+    def load():
+        for c in range(n):
+            for h in range(2):
+                q, p = axes(h)
+                pltpu.make_async_copy(
+                    t_hbm.at[pl.ds(h * HALF, HALF), pl.ds(STARTS[c], WIDTHS[c])], ts[c].at[block(h, q, p)], tsem.at[0]).start()
+        for cp in small:
+            cp.start()
+        tvcopy.start()
+        for first in (True, False):
+            for h in range(2):
+                for o in range(2):
+                    q, _ = axes(h)
+                    g = (q // 2 if first else 1 - q // 2) * 2 + o
+                    source = x_hbm.at[:, g, :, h] if h == 0 else x_hbm.at[:, :, g, h]
+                    pltpu.make_async_copy(source, xraw.at[h, g], xsem.at[1 - first]).start()
+            if first:
+                ucopy.start()
+        fcopy.start()
+
+    load()
     pl.semaphore_wait(bar, 8)
 
-    def send(c, h, kind, d, ref):
+    def send(c, h, kind, d, ref, source=None):
         q, p = axes(h)
         s = 1 if d == 0 else 3
         to = dev(h, p + s, q) if kind < 2 else dev(h, p, q + s)
         pltpu.make_async_remote_copy(
-            src_ref=ref, dst_ref=ref, send_sem=gs.at[c], recv_sem=gr.at[c * EVENTS + kind], device_id=to,
+            src_ref=ref if source is None else source, dst_ref=ref, send_sem=gs.at[c],
+            recv_sem=gr.at[c * EVENTS + kind], device_id=to,
             device_id_type=MESH).start()
 
     def arrived(c, kind, blocks):
@@ -112,12 +112,18 @@
     def src(v, d):
         return (v + (3 if d == 0 else 1)) % SIDE
 
-    def S(c):
-        for kind in (0, 2):
-            for h in range(2):
-                q, p = axes(h)
-                for d in range(2):
-                    send(c, h, kind, d, ts[c].at[block(h, q, p)])
+    def first_sends(c, kind):
+        for h in range(2):
+            q, p = axes(h)
+            for d in range(2):
+                send(c, h, kind, d, ts[c].at[block(h, q, p)],
+                     t_hbm.at[pl.ds(h * HALF, HALF), pl.ds(STARTS[c], WIDTHS[c])])
+
+    def D1(c):
+        first_sends(c, 0)
+
+    def O(c):
+        first_sends(c, 2)
 
     def E1(c):
         arrived(c, 0, 4)
@@ -125,6 +131,8 @@
             q, p = axes(h)
             for d in range(2):
                 send(c, h, 1, d, ts[c].at[block(h, q, src(p, d)), pl.ds(HALF // 2 * d, HALF // 2)])
+
+    def N(c):
         for k in range(2):
             for h in range(2):
                 q, p = axes(h)
@@ -174,12 +182,13 @@
             bd[i * OCC_J:(i + 1) * OCC_J, :] = jnp.where((lane >> 4) == i, tiled, 0.0).astype(BF)
         small[3].wait()
         tvcopy.wait()
+        pltpu.make_async_copy(t_hbm, tv, tsem.at[0]).wait()
         for b in range(VIRT // 128):
             piece = virt_v[:, b * 128:(b + 1) * 128].astype(F32)
             vcol[b * 128:(b + 1) * 128, :] = jnp.broadcast_to(piece, (128, 128)).T.astype(BF)
 
     def build(first):
-        pltpu.make_async_copy(x_hbm.at[pl.ds(0, ROWS // 2)], x_hbm.at[pl.ds(0, ROWS // 2)], xsem.at[1 - first]).wait()
+        pltpu.make_async_copy(xraw.at[0], xraw.at[0], xsem.at[1 - first]).wait()
         def body(b, _):
             h, o = b // 2, b % 2
             q = y + h * (x - y)
@@ -224,29 +233,30 @@
 
     def dots(c, groups, part=None):
         w = WIDTHS[c]
-        per = MT // OCC_J
+        size = ROWS // (2 if part is None else PARTS[c])
 
         def product(rows, h, start, count):
             ks = pl.ds(pl.multiple_of((h * SIDE + start) * SIDE * HALF, SIDE * HALF), count * SIDE * HALF)
             blocks = ts[c][pl.ds((h * SIDE + start) * SIDE, count * SIDE)].reshape(count * SIDE * HALF, w)
             return jnp.dot(xt[rows, ks], blocks, preferred_element_type=F32)
 
-        def body(mt, _):
-            rows = pl.ds(pl.multiple_of(mt * MT, MT), MT)
+        def body(step, _):
+            own = pl.ds(step * size, size)
+            rows = pl.ds(pl.multiple_of(step * size * OCC_J, size * OCC_J), size * OCC_J)
             if groups == 0:
                 total = jnp.dot(bd[rows, :], mid[:, STARTS[c]:STARTS[c] + w], preferred_element_type=F32)
             else:
-                total = accs[c][pl.ds(mt * per, per)].reshape(MT, w)
+                total = accs[c][own].reshape(size * OCC_J, w)
             for h in range(2):
                 q, _ = axes(h)
                 if groups < 2:
                     total = total + product(rows, h, (q // 2 if groups == 0 else 1 - q // 2) * 2, 2)
                 else:
                     total = total + product(rows, h, 3 - q if groups == 2 else (q + 2) % SIDE, 1)
-            accs[c][pl.ds(mt * per, per)] = total.reshape(per, SIDE, 2, COLS, w)
+            accs[c][own] = total.reshape(size, SIDE, 2, COLS, w)
             return 0
         if part is None:
-            lax.fori_loop(0, ROWS * OCC_J // MT, body, 0)
+            lax.fori_loop(0, 2, body, 0)
         else:
             body(part, 0)
 
@@ -257,7 +267,7 @@
     def to_sibling(c, part):
         i = share(c, part)
         return pltpu.make_async_remote_copy(
-            src_ref=s1s[c].at[i], dst_ref=r1s[c].at[i], send_sem=as_.at[2 * c + part], recv_sem=ar.at[2 * c + part],
+            src_ref=s1s[c].at[i], dst_ref=r1s[c].at[i], send_sem=as_.at[4 * c + part], recv_sem=ar.at[4 * c + part],
             device_id=sibling, device_id_type=MESH)
 
     def SA(c, part=0):
@@ -281,7 +291,7 @@
         pltpu.make_async_copy(finv.at[i, :, cols], fin_hbm.at[i, :, cols], osem.at[0]).start()
 
     for name, *args in SCHEDULE:
-        dict(S=S, E1=E1, E2=E2, G=G, H=H, prep=prep, build=build, middle=middle, onebody=onebody, dots=dots, SA=SA, SB=SB)[name](*args)
+        dict(D1=D1, O=O, E1=E1, N=N, E2=E2, G=G, H=H, prep=prep, build=build, middle=middle, onebody=onebody, dots=dots, SA=SA, SB=SB)[name](*args)
 
     for c in range(n):
         ref = ts[c].at[pl.ds(0, 30)]
@@ -311,7 +321,7 @@
     scratch += [vm((ROWS, SIDE, COLS, w), BF) for w in WIDTHS]
     scratch += [vm((ROWS, SIDE, COLS, w), BF) for w in WIDTHS]
     scratch += [vm((SIDE - 1, ROWS, COLS, w), BF) for w in WIDTHS]
-    scratch += [dma((k,)) for k in (1, 1, 2, 2, 1, 4, NCH, NCH * EVENTS, 2 * NCH, 2 * NCH, 1, 1)]
+    scratch += [dma((k,)) for k in (1, 1, 2, 2, 1, 4, NCH, NCH * EVENTS, 4 * NCH, 4 * NCH, 1, 1)]
     own, others = pl.pallas_call(
         kernel,
         out_shape=(jax.ShapeDtypeStruct((ROWS, COLS, VIRT), F32), jax.ShapeDtypeStruct((SIDE - 1, ROWS, COLS, VIRT), BF)),
@@ -320,7 +330,7 @@
         scratch_shapes=scratch,
         compiler_params=pltpu.CompilerParams(collective_id=0, has_side_effects=True, vmem_limit_bytes=60 * 2**20),
         name="residual",
-    )(amplitudes.reshape(ROWS * COLS, VIRT), hole_int.reshape(ROWS, OCC_I * COLS, OCC_J), ladder_int, cycle_virt,
+    )(amplitudes.reshape(ROWS * COLS, VIRT), hole_int.reshape(ROWS, SIDE, SIDE, 2, HALF, OCC_J), ladder_int, cycle_virt,
       cycle_occ, irrep_rows, irrep_cols.reshape(1, OCC_J), irrep_virt.reshape(1, VIRT))
     return (own + others[0].astype(F32) + others[1].astype(F32) + others[2].astype(F32)).astype(BF)
 

time: 57.1 us -> 55.4 us (0.970)
  Pallas kernels: 54.2 us -> 52.8 us
    pallas_call x1, Pallas kernels: 54.2 us -> 52.8 us  [local(): pl.pallas_call(kernel, out_shape=(jax.ShapeDtypeStruct((ROWS, COLS, VIRT)...]
where the time goes in v3:
time: 55.4 us; the launch traced here: 55.3 us
  Pallas kernels  52.8 us (95%)
  other arithmetic  2.46 us (4%)
    pallas_call x1, Pallas kernels, local(): pl.pallas_call(kernel, out_shape=(jax.ShapeDtypeStruct((ROWS, COLS, VIRT)...  52.8 us
    convert_element_type x1, other arithmetic, local(): (own + others[0].astype(F32) + others[1].astype(F32) + others[2].astype(F...  2.46 us

profile of v3, /device:TPU:1, one launch (start us, length us, event | category | flops | bytes accessed | tf_op | source)
XLA Modules:
  0.0 55.3 jit_solution(2845767937396081984)
XLA Ops:
  0.0 52.8 %residual.1 = (f32[12,16,1024]{2,1,0:T(8,128)}, bf16[3,12,16,1024]{3,2,1,0:T(8,128)(2,1)}) custom-call(bf16[192,1024]{1,0:T(8,128)(2,1)} %bitcast.14, bf16[12,4,4,2,96,128]{5,4,3,2,1,0:T(8,128)(2,1)} %bitcast.13, bf16[1024,1024]{1,0:T(8,128)(2,1)} %f_hbm.1, bf16[1024,1024]{1,0:T(8,128)(2,1)} %u_hbm.1, bf16[128,128]{1,0:T(8,128)(2,1)} %z_hbm.1, s32[192]{0:T(256)} %rows_hbm.1, ...), custom_call_target="tpu_custom_call" | custom-call | tf_op jit(solution)/shard_map/residual/pallas_call | solution.py:325
  52.8 2.5 %fusion = bf16[12,16,1024]{2,1,0:T(8,128)(2,1)} fusion(f32[12,16,1024]{2,1,0:T(8,128)} %get-tuple-element.7, bf16[3,12,16,1024]{3,2,1,0:T(8,128)(2,1)} %get-tuple-element.8), kind=kLoop, calls=%fused_computation.1 | loop fusion | flops 1376256 | bytes 2359296 | tf_op jit(solution)/shard_map/convert_element_type | solution.py:335

commit v4 on v3

--- a/solution.py
+++ b/solution.py
@@ -21,7 +21,7 @@
 
 
 SCHEDULE = (
-    ('D1', 0), ('O', 0), ('D1', 1), ('D1', 2), ('prep',), ('build', True), ('E1', 0), ('D1', 3), ('N', 0), ('middle',), ('E1', 1), ('E2', 0), ('N', 1), ('build', False), ('O', 1), ('G', 0, 3), ('G', 0, 4), ('G', 0, 2), ('onebody',), ('G', 0, 5), ('E2', 1), ('E1', 2), ('dots', 0, 0), ('O', 2), ('G', 1, 2), ('N', 2), ('G', 1, 3), ('G', 1, 4), ('H', 0), ('dots', 0, 1), ('G', 1, 5), ('E2', 2), ('SA', 0), ('E1', 3), ('dots', 1, 0), ('N', 3), ('SB', 0), ('G', 2, 3), ('G', 2, 4), ('G', 2, 2), ('H', 1), ('dots', 1, 1), ('G', 2, 5), ('O', 3), ('SA', 1), ('E2', 3), ('dots', 2, 0), ('G', 3, 4), ('G', 3, 3), ('SB', 1), ('H', 2), ('dots', 2, 1), ('G', 3, 2), ('SA', 2), ('G', 3, 5), ('dots', 3, 0), ('SB', 2), ('dots', 3, 2), ('H', 3), ('dots', 3, 3, 0), ('SA', 3, 0), ('dots', 3, 3, 1), ('SA', 3, 1), ('dots', 3, 3, 2), ('SA', 3, 2), ('dots', 3, 3, 3), ('SA', 3, 3), ('SB', 3, 0), ('SB', 3, 1), ('SB', 3, 2), ('SB', 3, 3),
+    ('D1', 0), ('O', 0), ('D1', 1), ('D1', 2), ('load_rest',), ('prep',), ('build', True), ('E1', 0), ('D1', 3), ('N', 0), ('middle',), ('E1', 1), ('E2', 0), ('N', 1), ('build', False), ('O', 1), ('G', 0, 3), ('G', 0, 4), ('G', 0, 2), ('onebody',), ('G', 0, 5), ('E2', 1), ('E1', 2), ('dots', 0, 0), ('O', 2), ('G', 1, 2), ('N', 2), ('G', 1, 3), ('G', 1, 4), ('H', 0), ('dots', 0, 1), ('G', 1, 5), ('E2', 2), ('SA', 0), ('E1', 3), ('dots', 1, 0), ('N', 3), ('SB', 0), ('G', 2, 3), ('G', 2, 4), ('G', 2, 2), ('H', 1), ('dots', 1, 1), ('G', 2, 5), ('O', 3), ('SA', 1), ('E2', 3), ('dots', 2, 0), ('G', 3, 4), ('G', 3, 3), ('SB', 1), ('H', 2), ('dots', 2, 1), ('G', 3, 2), ('SA', 2), ('G', 3, 5), ('dots', 3, 0), ('SB', 2), ('dots', 3, 2), ('H', 3), ('dots', 3, 3, 0), ('SA', 3, 0), ('dots', 3, 3, 1), ('SA', 3, 1), ('dots', 3, 3, 2), ('SA', 3, 2), ('dots', 3, 3, 3), ('SA', 3, 3), ('SB', 3, 0), ('SB', 3, 1), ('SB', 3, 2), ('SB', 3, 3),
 )
 
 
@@ -77,6 +77,8 @@
         for cp in small:
             cp.start()
         tvcopy.start()
+
+    def load_rest():
         for first in (True, False):
             for h in range(2):
                 for o in range(2):
@@ -291,7 +293,7 @@
         pltpu.make_async_copy(finv.at[i, :, cols], fin_hbm.at[i, :, cols], osem.at[0]).start()
 
     for name, *args in SCHEDULE:
-        dict(D1=D1, O=O, E1=E1, N=N, E2=E2, G=G, H=H, prep=prep, build=build, middle=middle, onebody=onebody, dots=dots, SA=SA, SB=SB)[name](*args)
+        dict(load_rest=load_rest, D1=D1, O=O, E1=E1, N=N, E2=E2, G=G, H=H, prep=prep, build=build, middle=middle, onebody=onebody, dots=dots, SA=SA, SB=SB)[name](*args)
 
     for c in range(n):
         ref = ts[c].at[pl.ds(0, 30)]

time: 55.4 us -> 54.9 us (level)
  no operation moved by 1% of the time
where the time goes in v4:
time: 54.9 us; the launch traced here: 54.7 us
  Pallas kernels  52.3 us (95%)
  other arithmetic  2.46 us (4%)
    pallas_call x1, Pallas kernels, local(): pl.pallas_call(kernel, out_shape=(jax.ShapeDtypeStruct((ROWS, COLS, VIRT)...  52.3 us
    convert_element_type x1, other arithmetic, local(): (own + others[0].astype(F32) + others[1].astype(F32) + others[2].astype(F...  2.46 us

profile of v4, /device:TPU:1, one launch (start us, length us, event | category | flops | bytes accessed | tf_op | source)
XLA Modules:
  0.0 54.7 jit_solution(10689308310722316556)
XLA Ops:
  0.0 52.3 %residual.1 = (f32[12,16,1024]{2,1,0:T(8,128)}, bf16[3,12,16,1024]{3,2,1,0:T(8,128)(2,1)}) custom-call(bf16[192,1024]{1,0:T(8,128)(2,1)} %bitcast.14, bf16[12,4,4,2,96,128]{5,4,3,2,1,0:T(8,128)(2,1)} %bitcast.13, bf16[1024,1024]{1,0:T(8,128)(2,1)} %f_hbm.1, bf16[1024,1024]{1,0:T(8,128)(2,1)} %u_hbm.1, bf16[128,128]{1,0:T(8,128)(2,1)} %z_hbm.1, s32[192]{0:T(256)} %rows_hbm.1, ...), custom_call_target="tpu_custom_call" | custom-call | tf_op jit(solution)/shard_map/residual/pallas_call | solution.py:327
  52.3 2.5 %fusion = bf16[12,16,1024]{2,1,0:T(8,128)(2,1)} fusion(f32[12,16,1024]{2,1,0:T(8,128)} %get-tuple-element.7, bf16[3,12,16,1024]{3,2,1,0:T(8,128)(2,1)} %get-tuple-element.8), kind=kLoop, calls=%fused_computation.1 | loop fusion | flops 1376256 | bytes 2359296 | tf_op jit(solution)/shard_map/convert_element_type | solution.py:337

commit v5 on v4

--- a/solution.py
+++ b/solution.py
@@ -269,7 +269,7 @@
     def to_sibling(c, part):
         i = share(c, part)
         return pltpu.make_async_remote_copy(
-            src_ref=s1s[c].at[i], dst_ref=r1s[c].at[i], send_sem=as_.at[4 * c + part], recv_sem=ar.at[4 * c + part],
+            src_ref=s1s[c].at[i], dst_ref=r1s[c].at[i], send_sem=as_.at[0], recv_sem=ar.at[c + part],
             device_id=sibling, device_id_type=MESH)
 
     def SA(c, part=0):
@@ -299,8 +299,8 @@
         ref = ts[c].at[pl.ds(0, 30)]
         pltpu.make_async_remote_copy(
             src_ref=ref, dst_ref=ref, send_sem=gs.at[c], recv_sem=gr.at[c], device_id=sibling, device_id_type=MESH).wait_send()
-        for part in range(PARTS[c]):
-            to_sibling(c, part).wait_send()
+    pltpu.make_async_remote_copy(
+        src_ref=ts[0], dst_ref=ts[0], send_sem=as_.at[0], recv_sem=ar.at[0], device_id=sibling, device_id_type=MESH).wait_send()
     pltpu.make_async_copy(finv, fin_hbm, osem.at[0]).wait()
     last = pltpu.make_async_remote_copy(
         src_ref=r2_hbm, dst_ref=r2_hbm, send_sem=bs.at[0], recv_sem=br.at[0], device_id=sibling, device_id_type=MESH)
@@ -323,7 +323,7 @@
     scratch += [vm((ROWS, SIDE, COLS, w), BF) for w in WIDTHS]
     scratch += [vm((ROWS, SIDE, COLS, w), BF) for w in WIDTHS]
     scratch += [vm((SIDE - 1, ROWS, COLS, w), BF) for w in WIDTHS]
-    scratch += [dma((k,)) for k in (1, 1, 2, 2, 1, 4, NCH, NCH * EVENTS, 4 * NCH, 4 * NCH, 1, 1)]
+    scratch += [dma((k,)) for k in (1, 1, 2, 2, 1, 4, NCH, NCH * EVENTS, 1, NCH + PARTS[-1], 1, 1)]
     own, others = pl.pallas_call(
         kernel,
         out_shape=(jax.ShapeDtypeStruct((ROWS, COLS, VIRT), F32), jax.ShapeDtypeStruct((SIDE - 1, ROWS, COLS, VIRT), BF)),

time: 54.9 us -> 54.7 us (level)
  no operation moved by 1% of the time
where the time goes in v5:
time: 54.7 us; the launch traced here: 54.5 us
  Pallas kernels  52.1 us (95%)
  other arithmetic  2.46 us (4%)
    pallas_call x1, Pallas kernels, local(): pl.pallas_call(kernel, out_shape=(jax.ShapeDtypeStruct((ROWS, COLS, VIRT)...  52.1 us
    convert_element_type x1, other arithmetic, local(): (own + others[0].astype(F32) + others[1].astype(F32) + others[2].astype(F...  2.46 us

profile of v5, /device:TPU:1, one launch (start us, length us, event | category | flops | bytes accessed | tf_op | source)
XLA Modules:
  0.0 54.5 jit_solution(730218051791909573)
XLA Ops:
  0.0 52.1 %residual.1 = (f32[12,16,1024]{2,1,0:T(8,128)}, bf16[3,12,16,1024]{3,2,1,0:T(8,128)(2,1)}) custom-call(bf16[192,1024]{1,0:T(8,128)(2,1)} %bitcast.14, bf16[12,4,4,2,96,128]{5,4,3,2,1,0:T(8,128)(2,1)} %bitcast.13, bf16[1024,1024]{1,0:T(8,128)(2,1)} %f_hbm.1, bf16[1024,1024]{1,0:T(8,128)(2,1)} %u_hbm.1, bf16[128,128]{1,0:T(8,128)(2,1)} %z_hbm.1, s32[192]{0:T(256)} %rows_hbm.1, ...), custom_call_target="tpu_custom_call" | custom-call | tf_op jit(solution)/shard_map/residual/pallas_call | solution.py:327
  52.1 2.5 %fusion = bf16[12,16,1024]{2,1,0:T(8,128)(2,1)} fusion(f32[12,16,1024]{2,1,0:T(8,128)} %get-tuple-element.7, bf16[3,12,16,1024]{3,2,1,0:T(8,128)(2,1)} %get-tuple-element.8), kind=kLoop, calls=%fused_computation.1 | loop fusion | flops 1376256 | bytes 2359296 | tf_op jit(solution)/shard_map/convert_element_type | solution.py:337

commit v6 on v5

--- a/solution.py
+++ b/solution.py
@@ -16,12 +16,12 @@
 WIDTHS = (256, 256, 256, 256)
 STARTS = tuple(sum(WIDTHS[:c]) for c in range(len(WIDTHS)))
 NCH = len(WIDTHS)
-PARTS = (1, 1, 1, 4)
+PARTS = (1, 1, 1, 6)
 EVENTS = 8
 
 
 SCHEDULE = (
-    ('D1', 0), ('O', 0), ('D1', 1), ('D1', 2), ('load_rest',), ('prep',), ('build', True), ('E1', 0), ('D1', 3), ('N', 0), ('middle',), ('E1', 1), ('E2', 0), ('N', 1), ('build', False), ('O', 1), ('G', 0, 3), ('G', 0, 4), ('G', 0, 2), ('onebody',), ('G', 0, 5), ('E2', 1), ('E1', 2), ('dots', 0, 0), ('O', 2), ('G', 1, 2), ('N', 2), ('G', 1, 3), ('G', 1, 4), ('H', 0), ('dots', 0, 1), ('G', 1, 5), ('E2', 2), ('SA', 0), ('E1', 3), ('dots', 1, 0), ('N', 3), ('SB', 0), ('G', 2, 3), ('G', 2, 4), ('G', 2, 2), ('H', 1), ('dots', 1, 1), ('G', 2, 5), ('O', 3), ('SA', 1), ('E2', 3), ('dots', 2, 0), ('G', 3, 4), ('G', 3, 3), ('SB', 1), ('H', 2), ('dots', 2, 1), ('G', 3, 2), ('SA', 2), ('G', 3, 5), ('dots', 3, 0), ('SB', 2), ('dots', 3, 2), ('H', 3), ('dots', 3, 3, 0), ('SA', 3, 0), ('dots', 3, 3, 1), ('SA', 3, 1), ('dots', 3, 3, 2), ('SA', 3, 2), ('dots', 3, 3, 3), ('SA', 3, 3), ('SB', 3, 0), ('SB', 3, 1), ('SB', 3, 2), ('SB', 3, 3),
+    ('D1', 0), ('O', 0), ('D1', 1), ('D1', 2), ('load_rest',), ('prep',), ('build', True), ('E1', 0), ('D1', 3), ('N', 0), ('middle',), ('E1', 1), ('E2', 0), ('N', 1), ('build', False), ('O', 1), ('G', 0, 3), ('G', 0, 4), ('G', 0, 2), ('onebody',), ('G', 0, 5), ('E2', 1), ('E1', 2), ('dots', 0, 0), ('O', 2), ('G', 1, 2), ('N', 2), ('G', 1, 3), ('G', 1, 4), ('H', 0), ('dots', 0, 1), ('G', 1, 5), ('E2', 2), ('SA', 0), ('E1', 3), ('dots', 1, 0), ('N', 3), ('SB', 0), ('G', 2, 3), ('G', 2, 4), ('G', 2, 2), ('H', 1), ('dots', 1, 1), ('G', 2, 5), ('O', 3), ('SA', 1), ('E2', 3), ('dots', 2, 0), ('G', 3, 4), ('G', 3, 3), ('SB', 1), ('H', 2), ('dots', 2, 1), ('G', 3, 2), ('SA', 2), ('G', 3, 5), ('dots', 3, 0), ('SB', 2), ('dots', 3, 2), ('H', 3), ('dots', 3, 3, 0), ('SA', 3, 0), ('dots', 3, 3, 1), ('SA', 3, 1), ('dots', 3, 3, 2), ('SA', 3, 2), ('dots', 3, 3, 3), ('SA', 3, 3), ('SB', 3, 0), ('dots', 3, 3, 4), ('SA', 3, 4), ('SB', 3, 1), ('dots', 3, 3, 5), ('SA', 3, 5), ('SB', 3, 2), ('SB', 3, 3), ('SB', 3, 4), ('SB', 3, 5),
 )
 
 
@@ -334,7 +334,22 @@
         name="residual",
     )(amplitudes.reshape(ROWS * COLS, VIRT), hole_int.reshape(ROWS, SIDE, SIDE, 2, HALF, OCC_J), ladder_int, cycle_virt,
       cycle_occ, irrep_rows, irrep_cols.reshape(1, OCC_J), irrep_virt.reshape(1, VIRT))
-    return (own + others[0].astype(F32) + others[1].astype(F32) + others[2].astype(F32)).astype(BF)
+    def final(own_ref, others_ref, out_ref):
+        total = own_ref[...]
+        for d in range(SIDE - 1):
+            total = total + others_ref[d].astype(F32)
+        out_ref[...] = total.astype(BF)
+
+    rows = pl.BlockSpec((ROWS // 2, COLS, VIRT), lambda i: (i, 0, 0))
+    return pl.pallas_call(
+        final,
+        grid=(2,),
+        out_shape=jax.ShapeDtypeStruct((ROWS, COLS, VIRT), BF),
+        in_specs=[rows, pl.BlockSpec((SIDE - 1, ROWS // 2, COLS, VIRT), lambda i: (0, i, 0, 0))],
+        out_specs=rows,
+        compiler_params=pltpu.CompilerParams(vmem_limit_bytes=60 * 2**20),
+        name="final",
+    )(own, others)
 
 
 def solution(mesh):

time: 54.7 us -> 54.5 us (level)
  other arithmetic: 2.46 us -> 0 us
  Pallas kernels: 52.1 us -> 54.4 us
    convert_element_type x1 -> x0, other arithmetic: 2.46 us -> none  [local(): (own + others[0].astype(F32) + others[1].astype(F32) + others[2].astype(F...]
    pallas_call x0 -> x1, Pallas kernels: none -> 2.27 us  [local(): pl.pallas_call(final, grid=(2,), out_shape=jax.ShapeDtypeStruct((ROWS, CO...]
where the time goes in v6:
time: 54.5 us; the launch traced here: 54.4 us
  Pallas kernels  54.4 us (100%)
    pallas_call x1, Pallas kernels, local(): pl.pallas_call(kernel, out_shape=(jax.ShapeDtypeStruct((ROWS, COLS, VIRT)...  52.1 us
    pallas_call x1, Pallas kernels, local(): pl.pallas_call(final, grid=(2,), out_shape=jax.ShapeDtypeStruct((ROWS, CO...  2.27 us

profile of v6, /device:TPU:1, one launch (start us, length us, event | category | flops | bytes accessed | tf_op | source)
XLA Modules:
  0.0 54.4 jit_solution(10925572235739718498)
XLA Ops:
  0.0 52.1 %residual.1 = (f32[12,16,1024]{2,1,0:T(8,128)}, bf16[3,12,16,1024]{3,2,1,0:T(8,128)(2,1)}) custom-call(bf16[192,1024]{1,0:T(8,128)(2,1)} %bitcast.5, bf16[12,4,4,2,96,128]{5,4,3,2,1,0:T(8,128)(2,1)} %bitcast.4, bf16[1024,1024]{1,0:T(8,128)(2,1)} %f_hbm.1, bf16[1024,1024]{1,0:T(8,128)(2,1)} %u_hbm.1, bf16[128,128]{1,0:T(8,128)(2,1)} %z_hbm.1, s32[192]{0:T(256)} %rows_hbm.1, ...), custom_call_target="tpu_custom_call" | custom-call | tf_op jit(solution)/shard_map/residual/pallas_call | solution.py:327
  52.1 2.3 %final.1 = bf16[12,16,1024]{2,1,0:T(8,128)(2,1)} custom-call(f32[12,16,1024]{2,1,0:T(8,128)} %get-tuple-element.7.own_ref, bf16[3,12,16,1024]{3,2,1,0:T(8,128)(2,1)} %get-tuple-element.8.others_ref), custom_call_target="tpu_custom_call" | custom-call | tf_op jit(solution)/shard_map/final/pallas_call | solution.py:344
